TPU v7x, 256 devices: a whole 4x4x8 slice. The times are simulated.
256 devices in a mesh: fluid: 64 (over x, z, core), metal: 4 (over y).
Axes of the slice: x: 4, y: 4, z: 8, core: 2. Of those that a mesh axis runs over, the one named last changes fastest.
Arguments:
- fluid_x: bfloat16 [16384, 512], P('fluid', 'metal'), may hold values from -32 to 32
- metal_x: bfloat16 [8192, 512], P('fluid', 'metal'), may hold values from -32 to 32
- w_rf: bfloat16 [512, 512], P(None, 'metal'), may hold values from -0.5 to 0.5
- w_vf: bfloat16 [512, 512], P(None, 'metal'), may hold values from -0.25 to 0.25
- w_rm: bfloat16 [512, 512], P(None, 'metal'), may hold values from -0.5 to 0.5
- w_vm: bfloat16 [512, 512], P(None, 'metal'), may hold values from -0.25 to 0.25
- fluid_grad: bfloat16 [16384, 512], P('fluid', 'metal'), may hold values from -6 to 6
- metal_grad: bfloat16 [8192, 512], P('fluid', 'metal'), may hold values from -6 to 6
- pair_list: int32 [2048, 2], P('fluid'), may hold values from 0 to 63, as said below
- pair_count: int32 [64], P('fluid'), may hold values from 2 to 32, as said below
Outputs:
- fluid_out: bfloat16 [16384, 512], P('fluid', 'metal')
- metal_out: bfloat16 [8192, 512], P('fluid', 'metal')
- fluid_dx: bfloat16 [16384, 512], P('fluid', 'metal')
- metal_dx: bfloat16 [8192, 512], P('fluid', 'metal')
- weight_grads: float32 [4, 512, 512], P(None, None, 'metal')
Inputs may be any that keep to these rules, and one draw needn't show every extreme that they name: `pair_list`: column 0 is a local fluid block below 2, column 1 a metal block below 64. The first pair_count[d] entries of fluid index d are distinct pairs; every fluid block of every index and every metal block stands in some live entry; entries past the count hold valid indices and are ignored. `pair_count`: some fluid index has all 32 slots live.
All inputs are finite; a program needn't handle non-finite values.
Results may differ from a plain program's by a relative error of at most 0.0179.
The roundings to bfloat16 on the way count: a program that leaves them out, or rounds other values in their place, can miss the bound.
Values may be sent and summed in bfloat16 or wider, within the bound.
No kernel may reach another device: no remote copies, remote signals or barrier semaphores. Data moves between devices by JAX's collectives and lax.ppermute only.
A program may use at most 128 MiB of HBM per device.

v0:
```python
import math
import jax
import jax.numpy as jnp
from jax import lax
from jax.sharding import PartitionSpec as P

D = 512
H = 8
BLK = 128
LOWEST = -1e30


def project(inputs, weight):
    return jnp.dot(inputs, weight, preferred_element_type=jnp.float32).astype(jnp.bfloat16)


def back_project(grads, weight):
    return lax.dot_general(
        grads, weight, (((1,), (1,)), ((), ())), preferred_element_type=jnp.float32
    )


def outer_rows(inputs, grads):
    return lax.dot_general(
        inputs, grads, (((0,), (0,)), ((), ())), preferred_element_type=jnp.float32
    )


def body(fluid_x, metal_x, w_rf, w_vf, w_rm, w_vm, fluid_grad, metal_grad, pair_list, pair_count):
    head_size = D // H
    local_heads = w_rf.shape[1] // head_size
    feature_cols = w_rf.shape[1]
    fluid_rows = fluid_x.shape[0]
    blocks = fluid_rows // BLK
    metal_blocks = lax.axis_size("fluid")
    metal_rows = metal_blocks * BLK
    slot_total = pair_list.shape[0]
    batch_size = math.gcd(slot_total, 16)
    inv_root = 1.0 / math.sqrt(head_size)
    live_count = pair_count[0]
    loop_turns = slot_total // batch_size
    fluid_full, metal_full = (
        lax.all_gather(fluid_x, "metal", axis=1, tiled=True),
        lax.all_gather(metal_x, "metal", axis=1, tiled=True),
    )
    fluid_keys = project(fluid_full, w_rf)
    fluid_values = project(fluid_full, w_vf)
    metal_keys = project(metal_full, w_rm)
    metal_values = project(metal_full, w_vm)
    keys_all, values_all = (
        lax.all_gather(metal_keys, "fluid", axis=0, tiled=True),
        lax.all_gather(metal_values, "fluid", axis=0, tiled=True),
    )
    fkey_tiles = fluid_keys.reshape(blocks, BLK, local_heads, head_size)
    fval_tiles = fluid_values.reshape(blocks, BLK, local_heads, head_size)
    mkey_tiles = keys_all.reshape(metal_blocks, BLK, local_heads, head_size)
    mval_tiles = values_all.reshape(metal_blocks, BLK, local_heads, head_size)

    def batch_pairs(number):
        entries = lax.dynamic_slice_in_dim(pair_list, number * batch_size, batch_size, 0)
        slot_index = number * batch_size + jnp.arange(batch_size, dtype=jnp.int32)
        frows = entries[:, 0]
        mrows = entries[:, 1]
        scores = (
            jnp.einsum(
                "pahd,pbhd->phab",
                fkey_tiles[frows],
                mkey_tiles[mrows],
                preferred_element_type=jnp.float32,
            )
            * inv_root
        )
        return (frows, mrows, slot_index < live_count, scores)

    def max_pass(number, state):
        row_max, col_max = state
        frows, mrows, active, scores = batch_pairs(number)
        live = active[:, None, None]
        row_max = row_max.at[frows].max(jnp.where(live, jnp.max(scores, axis=3), LOWEST))
        col_max = col_max.at[mrows].max(jnp.where(live, jnp.max(scores, axis=2), LOWEST))
        return (row_max, col_max)

    row_max, col_local = lax.fori_loop(
        0,
        loop_turns,
        max_pass,
        (
            jnp.full((blocks, local_heads, BLK), LOWEST, jnp.float32),
            jnp.full((metal_blocks, local_heads, BLK), LOWEST, jnp.float32),
        ),
    )
    col_max = lax.pmax(col_local, "fluid")

    def sum_pass(number, state):
        row_sum, fluid_num, col_sum, metal_num = state
        frows, mrows, active, scores = batch_pairs(number)
        live = active[:, None, None, None]
        row_exp = jnp.where(live, jnp.exp(scores - row_max[frows][:, :, :, None]), 0.0)
        col_exp = jnp.where(live, jnp.exp(scores - col_max[mrows][:, :, None, :]), 0.0)
        row_sum = row_sum.at[frows].add(jnp.sum(row_exp, axis=3))
        col_sum = col_sum.at[mrows].add(jnp.sum(col_exp, axis=2))
        fluid_num = fluid_num.at[frows].add(
            jnp.einsum(
                "phab,pbhd->pahd",
                row_exp.astype(jnp.bfloat16),
                mval_tiles[mrows],
                preferred_element_type=jnp.float32,
            )
        )
        metal_num = metal_num.at[mrows].add(
            jnp.einsum(
                "phab,pahd->pbhd",
                col_exp.astype(jnp.bfloat16),
                fval_tiles[frows],
                preferred_element_type=jnp.float32,
            )
        )
        return (row_sum, fluid_num, col_sum, metal_num)

    row_sum, fluid_num, col_sum, metal_num = lax.fori_loop(
        0,
        loop_turns,
        sum_pass,
        (
            jnp.zeros((blocks, local_heads, BLK), jnp.float32),
            jnp.zeros((blocks, BLK, local_heads, head_size), jnp.float32),
            jnp.zeros((metal_blocks, local_heads, BLK), jnp.float32),
            jnp.zeros((metal_blocks, BLK, local_heads, head_size), jnp.float32),
        ),
    )
    fluid_out = (
        (fluid_num / row_sum.transpose(0, 2, 1)[:, :, :, None])
        .reshape(fluid_rows, feature_cols)
        .astype(jnp.bfloat16)
    )
    num_rows = metal_num.reshape(metal_rows, feature_cols)
    total_rows = col_sum.transpose(0, 2, 1).reshape(metal_rows, local_heads)
    own_num, own_sum = (
        lax.psum_scatter(num_rows, "fluid", scatter_dimension=0, tiled=True),
        lax.psum_scatter(total_rows, "fluid", scatter_dimension=0, tiled=True),
    )
    metal_out = (
        (own_num.reshape(BLK, local_heads, head_size) / own_sum[:, :, None])
        .reshape(BLK, feature_cols)
        .astype(jnp.bfloat16)
    )
    scaled_grad = (
        (metal_grad.astype(jnp.float32).reshape(BLK, local_heads, head_size) / own_sum[:, :, None])
        .reshape(BLK, feature_cols)
        .astype(jnp.bfloat16)
    )
    scaled_all, output_all = (
        lax.all_gather(scaled_grad, "fluid", axis=0, tiled=True),
        lax.all_gather(metal_out, "fluid", axis=0, tiled=True),
    )
    delta_f = jnp.sum(
        (fluid_grad.astype(jnp.float32) * fluid_out.astype(jnp.float32)).reshape(
            fluid_rows, local_heads, head_size
        ),
        axis=2,
    )
    delta_m = jnp.sum(
        (scaled_all.astype(jnp.float32) * output_all.astype(jnp.float32)).reshape(
            metal_blocks, BLK, local_heads, head_size
        ),
        axis=3,
    )
    grad_tiles = fluid_grad.reshape(blocks, BLK, local_heads, head_size)
    scaled_tiles = scaled_all.reshape(metal_blocks, BLK, local_heads, head_size)
    dfluid_tiles = delta_f.reshape(blocks, BLK, local_heads)

    def grad_pass(number, state):
        grad_rf, grad_vf, grad_rm, grad_vm = state
        frows, mrows, active, scores = batch_pairs(number)
        live = active[:, None, None, None]
        attn = jnp.where(
            live,
            jnp.exp(scores - row_max[frows][:, :, :, None]) / row_sum[frows][:, :, :, None],
            0.0,
        )
        col_exp = jnp.where(live, jnp.exp(scores - col_max[mrows][:, :, None, :]), 0.0)
        fluid_term = jnp.einsum(
            "pahd,pbhd->phab",
            grad_tiles[frows],
            mval_tiles[mrows],
            preferred_element_type=jnp.float32,
        )
        metal_term = jnp.einsum(
            "pahd,pbhd->phab",
            fval_tiles[frows],
            scaled_tiles[mrows],
            preferred_element_type=jnp.float32,
        )
        dscore = attn * (fluid_term - dfluid_tiles[frows].transpose(0, 2, 1)[:, :, :, None])
        dscore = dscore + col_exp * (metal_term - delta_m[mrows].transpose(0, 2, 1)[:, :, None, :])
        dscore_weight = dscore.astype(jnp.bfloat16)
        grad_rf = grad_rf.at[frows].add(
            jnp.einsum(
                "phab,pbhd->pahd",
                dscore_weight,
                mkey_tiles[mrows],
                preferred_element_type=jnp.float32,
            )
            * inv_root
        )
        grad_vf = grad_vf.at[frows].add(
            jnp.einsum(
                "phab,pbhd->pahd",
                col_exp.astype(jnp.bfloat16),
                scaled_tiles[mrows],
                preferred_element_type=jnp.float32,
            )
        )
        grad_rm = grad_rm.at[mrows].add(
            jnp.einsum(
                "phab,pahd->pbhd",
                dscore_weight,
                fkey_tiles[frows],
                preferred_element_type=jnp.float32,
            )
            * inv_root
        )
        grad_vm = grad_vm.at[mrows].add(
            jnp.einsum(
                "phab,pahd->pbhd",
                attn.astype(jnp.bfloat16),
                grad_tiles[frows],
                preferred_element_type=jnp.float32,
            )
        )
        return (grad_rf, grad_vf, grad_rm, grad_vm)

    grad_rf, grad_vf, grad_rm, grad_vm = lax.fori_loop(
        0,
        loop_turns,
        grad_pass,
        (
            jnp.zeros((blocks, BLK, local_heads, head_size), jnp.float32),
            jnp.zeros((blocks, BLK, local_heads, head_size), jnp.float32),
            jnp.zeros((metal_blocks, BLK, local_heads, head_size), jnp.float32),
            jnp.zeros((metal_blocks, BLK, local_heads, head_size), jnp.float32),
        ),
    )
    rf_rounded = grad_rf.reshape(fluid_rows, feature_cols).astype(jnp.bfloat16)
    vf_rounded = grad_vf.reshape(fluid_rows, feature_cols).astype(jnp.bfloat16)
    fluid_part = back_project(rf_rounded, w_rf) + back_project(vf_rounded, w_vf)
    fluid_part, weight_rf, weight_vf = (
        fluid_part,
        outer_rows(fluid_full, rf_rounded),
        outer_rows(fluid_full, vf_rounded),
    )
    rm_rounded = lax.psum_scatter(
        grad_rm.reshape(metal_rows, feature_cols), "fluid", scatter_dimension=0, tiled=True
    ).astype(jnp.bfloat16)
    vm_rounded = lax.psum_scatter(
        grad_vm.reshape(metal_rows, feature_cols), "fluid", scatter_dimension=0, tiled=True
    ).astype(jnp.bfloat16)
    metal_part = back_project(rm_rounded, w_rm) + back_project(vm_rounded, w_vm)
    weight_rm = outer_rows(metal_full, rm_rounded)
    weight_vm = outer_rows(metal_full, vm_rounded)
    fluid_dx, metal_dx = (
        lax.psum_scatter(fluid_part, "metal", scatter_dimension=1, tiled=True),
        lax.psum_scatter(metal_part, "metal", scatter_dimension=1, tiled=True),
    )
    weight_grads = lax.psum(jnp.stack([weight_rf, weight_vf, weight_rm, weight_vm]), "fluid")
    return (
        fluid_out,
        metal_out,
        fluid_dx.astype(jnp.bfloat16),
        metal_dx.astype(jnp.bfloat16),
        weight_grads,
    )


def solution(mesh):
    placed = (
        P("fluid", "metal"),
        P("fluid", "metal"),
        P(None, "metal"),
        P(None, "metal"),
        P(None, "metal"),
        P(None, "metal"),
        P("fluid", "metal"),
        P("fluid", "metal"),
        P("fluid", None),
        P("fluid"),
    )
    return jax.shard_map(
        body,
        mesh=mesh,
        in_specs=placed,
        out_specs=(
            P("fluid", "metal"),
            P("fluid", "metal"),
            P("fluid", "metal"),
            P("fluid", "metal"),
            P(None, None, "metal"),
        ),
        check_vma=False,
    )
```

profile of v0, /device:TPU:2, one launch (start us, length us, event | category | flops | bytes accessed | tf_op | source)
XLA Modules:
  0.0 1555.2 jit_solution(13822160661187020611)
XLA Ops:
  7.2 11.8 all_gather.19
  22.6 11.7 all_gather.18
  34.7 64.7 %all-gather.5.cloned.1.call-done = bf16[8192,128]{1,0:T(8,128)(2,1)} async-done(((bf16[128,128]{1,0:T(8,128)(2,1)}), bf16[8192,128]{1,0:T(8,128)(2,1)}) %all-gather.5.cloned.1.call-update) | async-done | bytes 2097168 | tf_op jit(solution)/shard_map/all_gather | solution.py:51
  99.4 8.2 reshape.334
  107.6 23.2 %while.53 = (s32[]{:T(128)}, f32[2,2,128]{2,1,0:T(2,128)S(1)}, f32[64,2,128]{2,1,0:T(2,128)S(1)}, s32[32,2]{0,1:T(2,128)S(1)}, s32[]{:T(128)}, /*index=5*/bf16[2...) while((s32[]{:T(128)}, f32[2,2,128]{2,1,0:T(2,128)S(1)}, ...), condition=%wide.region_5.6_spmd, body=%wide.region_0.5_spmd.sunk | while | flops 68692104 | bytes 3351623 | solution.py:83
  108.4 4.8 gather_fusion
  113.3 2.7 gather_fusion.1
  120.0 4.8 gather_fusion
  124.9 2.7 gather_fusion.1
  131.9 45.8 %all-gather.7.cloned.1.call-done = bf16[8192,128]{1,0:T(8,128)(2,1)} async-done(((bf16[128,128]{1,0:T(8,128)(2,1)}), bf16[8192,128]{1,0:T(8,128)(2,1)}) %all-gather.7.cloned.1.call-update) | async-done | bytes 2097168 | tf_op jit(solution)/shard_map/all_gather | solution.py:52
  177.7 8.3 reshape.335
  185.9 161.9 %all-reduce.3.cloned.1.call-done = f32[64,2,128]{2,1,0:T(2,128)} async-done(((f32[64,2,128]{2,1,0:T(2,128)}), f32[64,2,128]{2,1,0:T(2,128)}) %all-reduce.3.cloned.1.call-update) | async-done | bytes 65552 | tf_op jit(solution)/shard_map/pmax | solution.py:92
  350.3 67.5 %while.54 = (s32[]{:T(128)}, f32[2,2,128]{2,1,0:T(2,128)S(1)}, f32[2,128,2,64]{1,3,2,0:T(8,128)S(1)}, f32[64,2,128]{2,1,0:T(2,128)S(1)}, f32[64,128,2,64]{1,3,2,...) while((s32[]{:T(128)}, f32[2,2,128]{2,1,0:T(2,128)S(1)}, ...), condition=%wide.region_14.15_spmd, body=%wide.region_7.14_spmd.sunk | while | flops 209717376 | bytes 25437748 | solution.py:120
  353.3 4.8 gather_fusion.6
  358.2 5.7 gather_fusion.4
  363.9 2.7 gather_fusion.7
  366.6 3.6 gather_fusion.5
  370.2 3.2 fusion.127
  380.6 3.4 scatter_fusion.5
  386.7 4.8 gather_fusion.6
  391.6 5.7 gather_fusion.4
  397.3 2.7 gather_fusion.7
  400.0 3.6 gather_fusion.5
  403.6 3.2 fusion.127
  414.0 3.4 scatter_fusion.5
  417.9 2.7 copy.124
  420.6 4.6 copy.105
  425.2 5.2 copy.186
  431.3 130.0 %reduce-scatter.19.cloned.1.call-done = f32[128,2]{1,0:T(8,128)} async-done(((f32[8192,2]{1,0:T(8,128)}), f32[128,2]{1,0:T(8,128)}) %reduce-scatter.19.cloned.1.call-update) | async-done | bytes 1040
  562.2 145.2 %reduce-scatter.9.cloned.1.call-done = f32[128,128]{0,1:T(8,128)} async-done(((f32[8192,128]{0,1:T(8,128)}), f32[128,128]{0,1:T(8,128)}) %reduce-scatter.9.cloned.1.call-update) | async-done | bytes 65552 | tf_op jit(solution)/shard_map/reduce_scatter | solution.py:139
  710.1 72.3 %all-gather.9.cloned.1.call-done = bf16[8192,128]{0,1:T(8,128)(2,1)} async-done(((bf16[128,128]{0,1:T(8,128)(2,1)}), bf16[8192,128]{0,1:T(8,128)(2,1)}) %all-gather.9.cloned.1.call-update) | async-done | bytes 2097168 | tf_op jit(solution)/shard_map/all_gather | solution.py:153
  782.4 74.9 %all-gather.11.cloned.1.call-done = bf16[8192,128]{0,1:T(8,128)(2,1)} async-done(((bf16[128,128]{0,1:T(8,128)(2,1)}), bf16[8192,128]{0,1:T(8,128)(2,1)}) %all-gather.11.cloned.1.call-update) | async-done | bytes 2097168 | tf_op jit(solution)/shard_map/all_gather | solution.py:154
  857.2 2.7 multiply_bitcast_fusion
  860.0 2.7 copy.133
  867.4 5.2 copy.114
  877.5 131.7 %while.55 = (s32[]{:T(128)}, f32[2,128,2,64]{1,3,2,0:T(8,128)S(1)}, f32[2,128,2,64]{1,3,2,0:T(8,128)S(1)}, f32[64,128,2,64]{1,3,2,0:T(8,128)}, f32[64,128,2,64]{...) while((s32[]{:T(128)}, f32[2,128,2,64]{1,3,2,0:T(8,128)S(1)}, ...), condition=%wide.region_24.25_spmd, body=%wide.region_19.24_spmd.sunk | while | flops 482347136 | bytes 61189336 | solution.py:233
  883.9 4.8 gather_fusion.11
  890.5 4.8 gather_fusion.10
  895.4 5.7 gather_fusion.8
  903.5 3.6 gather_fusion.13
  907.0 3.6 gather_fusion.12
  913.0 3.6 gather_fusion.9
  923.3 2.9 convolution_bitcast_fusion.15
  928.1 2.6 scatter_fusion.7
  936.5 3.4 scatter_fusion.8
  939.9 3.4 scatter_fusion.9
  949.6 4.8 gather_fusion.11
  956.2 4.8 gather_fusion.10
  961.1 5.7 gather_fusion.8
  969.2 3.6 gather_fusion.13
  972.7 3.6 gather_fusion.12
  978.7 3.6 gather_fusion.9
  989.0 2.9 convolution_bitcast_fusion.15
  1002.3 3.4 scatter_fusion.8
  1005.7 3.4 scatter_fusion.9
  1009.2 4.6 copy.119
  1013.9 5.2 copy.184
  1019.1 4.6 copy.118
  1023.8 5.3 copy.185
  1031.5 129.8 %reduce-scatter.15.cloned.1.call-done = f32[128,128]{0,1:T(8,128)} async-done(((f32[8192,128]{0,1:T(8,128)}), f32[128,128]{0,1:T(8,128)}) %reduce-scatter.15.cloned.1.call-update) | async-done | bytes 65552 | tf_op jit(solution)/shard_map/reduce_scatter | solution.py:255
  1162.3 145.3 %reduce-scatter.13.cloned.1.call-done = f32[128,128]{0,1:T(8,128)} async-done(((f32[8192,128]{0,1:T(8,128)}), f32[128,128]{0,1:T(8,128)}) %reduce-scatter.13.cloned.1.call-update) | async-done | bytes 65552 | tf_op jit(solution)/shard_map/reduce_scatter | solution.py:252
  1312.6 20.7 %reduce-scatter.11.cloned.1.call-done = f32[256,128]{1,0:T(8,128)} async-done(((f32[256,512]{1,0:T(8,128)}), f32[256,128]{1,0:T(8,128)}) %reduce-scatter.11.cloned.1.call-update) | async-done | bytes 131088 | tf_op jit(solution)/shard_map/reduce_scatter | solution.py:262
  1334.8 188.6 %all-reduce.5.cloned.1.call-done = f32[4,512,128]{1,2,0:T(8,128)} async-done(((f32[4,512,128]{1,2,0:T(8,128)}), f32[4,512,128]{1,2,0:T(8,128)}) %all-reduce.5.cloned.1.call-update) | async-done | bytes 1048592 | tf_op jit(solution)/shard_map/psum | solution.py:265
  1525.9 20.6 %reduce-scatter.17.cloned.1.call-done = f32[128,128]{1,0:T(8,128)} async-done(((f32[128,512]{1,0:T(8,128)}), f32[128,128]{1,0:T(8,128)}) %reduce-scatter.17.cloned.1.call-update) | async-done | bytes 65552 | tf_op jit(solution)/shard_map/reduce_scatter | solution.py:263
  (229 shorter events, 120.1 us)
Async XLA Ops:
  7.2 27.2 %copy-start = (bf16[512,128]{1,0:T(8,128)(2,1)S(1)}, bf16[512,128]{1,0:T(8,128)(2,1)}, u32[]{:S(2)}) copy-start(bf16[512,128]{1,0:T(8,128)(2,1)} %param.18) | copy-start | bytes 393220
  7.2 92.2 %all-gather.5.cloned.1.call-start = ((), (), s32[]{:S(2)}) async-start(), calls=%async_computation.6 | async-start | bytes 2129920 | tf_op jit(solution)/shard_map/all_gather | solution.py:51
  19.0 15.3 copy-start.8
  20.8 156.9 %all-gather.7.cloned.1.call-start = ((), (), s32[]{:S(2)}) async-start(), calls=%async_computation.7 | async-start | bytes 2129920 | tf_op jit(solution)/shard_map/all_gather | solution.py:52
  22.6 325.3 %all-reduce.3.cloned.1.call-start = ((), (), s32[]{:S(2)}) async-start(), calls=%async_computation.8 | async-start | bytes 131072 | tf_op jit(solution)/shard_map/pmax | solution.py:92
  34.3 97.2 %copy-start.6 = (bf16[256,512]{1,0:T(8,128)(2,1)}, bf16[256,512]{1,0:T(8,128)(2,1)S(1)}, u32[]{:S(2)}) copy-start(bf16[256,512]{1,0:T(8,128)(2,1)S(1)} %all_gather.18) | copy-start | bytes 786436
  34.7 72.9 %copy-start.22 = (s32[32,2]{0,1:T(2,128)S(1)}, s32[32,2]{0,1:T(2,128)}, u32[]{:S(2)}) copy-start(s32[32,2]{0,1:T(2,128)} %param.24) | copy-start | bytes 772
  107.6 24.0 %copy-start.13 = (bf16[512,128]{1,0:T(8,128)(2,1)S(1)}, bf16[512,128]{1,0:T(8,128)(2,1)}, u32[]{:S(2)}) copy-start(bf16[512,128]{1,0:T(8,128)(2,1)} %param.19) | copy-start | bytes 393220
  130.9 0.6 copy-start.10
  131.5 429.8 %reduce-scatter.19.cloned.1.call-start = ((), (), s32[]{:S(2)}) async-start(), calls=%async_computation.17 | async-start | bytes 4259840
  376.7 3.9 copy-start.1
  410.1 3.9 copy-start.1
  420.5 286.9 %reduce-scatter.9.cloned.1.call-start = ((), (), s32[]{:S(2)}) async-start(), calls=%async_computation.9 | async-start | bytes 4259840 | tf_op jit(solution)/shard_map/reduce_scatter | solution.py:139
  430.4 0.8 copy-start.27
  430.4 279.3 %copy-start.20 = (bf16[256,128]{1,0:T(8,128)(2,1)S(1)}, bf16[256,128]{1,0:T(8,128)(2,1)}, u32[]{:S(2)}) copy-start(bf16[256,128]{1,0:T(8,128)(2,1)} %param.22) | copy-start | bytes 196612
  430.5 351.9 %all-gather.9.cloned.1.call-start = ((), (), s32[]{:S(2)}) async-start(), calls=%async_computation.10 | async-start | bytes 2129920 | tf_op jit(solution)/shard_map/all_gather | solution.py:153
  708.9 148.3 %all-gather.11.cloned.1.call-start = ((), (), s32[]{:S(2)}) async-start(), calls=%async_computation.11 | async-start | bytes 2129920 | tf_op jit(solution)/shard_map/all_gather | solution.py:154
  709.7 451.6 %reduce-scatter.15.cloned.1.call-start = ((), (), s32[]{:S(2)}) async-start(), calls=%async_computation.14 | async-start | bytes 4259840 | tf_op jit(solution)/shard_map/reduce_scatter | solution.py:255
  710.0 149.9 %copy-start.11 = (bf16[2,128,2,64]{1,0,3,2:T(2,128)(2,1)}, bf16[2,128,2,64]{1,0,3,2:T(2,128)(2,1)S(1)}, u32[]{:S(2)}) copy-start(bf16[2,128,2,64]{1,0,3,2:T(2,128)(2,1)S(1)} %copy.104) | copy-start | bytes 196612
  878.9 0.6 copy-start.23
  878.9 0.6 copy-start.25
  919.8 1.0 copy-start.3
  919.8 1.4 copy-start.4
  919.8 1.4 copy-start.17
  919.8 1.4 copy-start.28
  926.2 1.9 copy-start.26
  933.9 2.6 copy-start.2
  933.9 2.6 copy-start.24
  936.5 3.4 copy-start.5
  944.6 0.6 copy-start.23
  944.6 0.6 copy-start.25
  985.5 1.0 copy-start.3
  985.5 1.4 copy-start.4
  985.5 1.4 copy-start.17
  985.5 1.4 copy-start.28
  991.9 1.9 copy-start.26
  999.6 2.6 copy-start.2
  999.6 2.6 copy-start.24
  1002.2 3.4 copy-start.5
  1019.1 288.5 %reduce-scatter.13.cloned.1.call-start = ((), (), s32[]{:S(2)}) async-start(), calls=%async_computation.13 | async-start | bytes 4259840 | tf_op jit(solution)/shard_map/reduce_scatter | solution.py:252
  1029.0 0.9 copy-start.14
  1029.0 2.0 copy-start.7
  1029.1 304.2 %reduce-scatter.11.cloned.1.call-start = ((), (), s32[]{:S(2)}) async-start(), calls=%async_computation.12 | async-start | bytes 655360 | tf_op jit(solution)/shard_map/reduce_scatter | solution.py:262
  1029.1 132.1 %copy-start.9 = (bf16[128,512]{1,0:T(8,128)(2,1)S(1)}, bf16[128,512]{1,0:T(8,128)(2,1)}, u32[]{:S(2)}) copy-start(bf16[128,512]{1,0:T(8,128)(2,1)} %copy-done.8) | copy-start | bytes 393220
  1031.0 492.3 %all-reduce.5.cloned.1.call-start = ((), (), s32[]{:S(2)}) async-start(), calls=%async_computation.16 | async-start | bytes 2097152 | tf_op jit(solution)/shard_map/psum | solution.py:265
  1031.5 278.4 %copy-start.15 = (bf16[512,128]{1,0:T(8,128)(2,1)S(1)}, bf16[512,128]{1,0:T(8,128)(2,1)}, u32[]{:S(2)}) copy-start(bf16[512,128]{1,0:T(8,128)(2,1)} %param.20) | copy-start | bytes 393220
  1162.3 147.8 %copy-start.16 = (bf16[512,128]{1,0:T(8,128)(2,1)S(1)}, bf16[512,128]{1,0:T(8,128)(2,1)}, u32[]{:S(2)}) copy-start(bf16[512,128]{1,0:T(8,128)(2,1)} %param.21) | copy-start | bytes 393220
  1162.3 147.8 %copy-start.21 = (f32[128,128]{0,1:T(8,128)S(1)}, f32[128,128]{0,1:T(8,128)}, u32[]{:S(2)}) copy-start(f32[128,128]{0,1:T(8,128)} %reduce-scatter.15.cloned.1.call-done) | copy-start | bytes 196612
  1307.6 2.3 copy-start.19
  1308.7 2.4 copy-start.12
  1308.7 3.1 copy-start.18
  1309.8 236.7 %reduce-scatter.17.cloned.1.call-start = ((), (), s32[]{:S(2)}) async-start(), calls=%async_computation.15 | async-start | bytes 327680 | tf_op jit(solution)/shard_map/reduce_scatter | solution.py:263
Sparse Core Ops, SparseCore 0:
  20.9 78.4 all-gather.4
  102.7 74.9 all-gather.6
  181.8 166.0 all-reduce.2
  420.7 140.5 reduce-scatter.18
  565.3 142.0 reduce-scatter.8
  710.7 71.6 all-gather.8
  785.8 71.3 all-gather.10
  1019.2 141.9 reduce-scatter.14
  1165.4 142.1 reduce-scatter.12
  1310.2 23.0 reduce-scatter.10
  1337.7 185.6 all-reduce.4
  1525.7 20.7 reduce-scatter.16
where the time goes:
time: 1570 us; the launch traced here: 1560 us
  waiting for transfers between devices  1200 us (76%)
  local copies, waits for them, and re-layouts  209 us (13%)
  other arithmetic  58.9 us (4%)
  matrix products  46.7 us (3%)
  blocking collectives  23.5 us (1%)
    psum x1, waiting for transfers between devices, body(): lax.psum(jnp.stack([weight_rf, weight_vf, weight_rm, weight_vm]), 'fluid')  189 us
    pmax x1, waiting for transfers between devices, body(): col_max = lax.pmax(col_local, 'fluid')  162 us
    reduce_scatter x1, waiting for transfers between devices, body(): lax.psum_scatter(grad_rm.reshape(metal_rows, feature_cols), 'fluid', scat...  145 us
    reduce_scatter x1, waiting for transfers between devices, body(): lax.psum_scatter(num_rows, 'fluid', scatter_dimension=0, tiled=True)  145 us
    unnamed x13, waiting for transfers between devices  131 us
    reduce_scatter x1, waiting for transfers between devices, body(): lax.psum_scatter(grad_vm.reshape(metal_rows, feature_cols), 'fluid', scat...  130 us
    all_gather x1, waiting for transfers between devices, body(): lax.all_gather(metal_out, 'fluid', axis=0, tiled=True)  74.9 us
    all_gather x1, waiting for transfers between devices, body(): lax.all_gather(scaled_grad, 'fluid', axis=0, tiled=True)  72.3 us
  transfers between devices with their start and end apart: 12, of which 12 were waited for; matrix products, arithmetic and copies ran while one was open for 5% of the time, Pallas kernels for 0%

commit v1 on v0

--- a/solution.py
+++ b/solution.py
@@ -8,6 +8,21 @@
 H = 8
 BLK = 128
 LOWEST = -1e30
+
+
+def halves_find(u, shard_axis, array_dim=0):
+    p_next = lax.axis_size(shard_axis)
+    part_next = lax.axis_index(shard_axis)
+    v_next, back, z2 = (p_next, part_next, u.shape[array_dim])
+    value_now, far_arr = (u, 1)
+    while far_arr < v_next:
+        state_now = lax.ppermute(
+            value_now, shard_axis, [(dev_j, (dev_j - far_arr) % v_next) for dev_j in range(v_next)]
+        )
+        value_now = jnp.concatenate([value_now, state_now], axis=array_dim)
+        far_arr = 2 * far_arr
+    passed = jnp.roll(value_now, shift=back * z2, axis=array_dim)
+    return passed
 
 
 def project(inputs, weight):
@@ -48,7 +63,7 @@
     metal_keys = project(metal_full, w_rm)
     metal_values = project(metal_full, w_vm)
     keys_all, values_all = (
-        lax.all_gather(metal_keys, "fluid", axis=0, tiled=True),
+        halves_find(metal_keys, "fluid"),
         lax.all_gather(metal_values, "fluid", axis=0, tiled=True),
     )
     fkey_tiles = fluid_keys.reshape(blocks, BLK, local_heads, head_size)

time: 1570 us -> 1540 us (0.981)
  waiting for transfers between devices: 1200 us -> 1160 us
    all_gather x1 -> x0, waiting for transfers between devices: 64.7 us -> none  [body(): lax.all_gather(metal_keys, 'fluid', axis=0, tiled=True)]
    ppermute x0 -> x6, waiting for transfers between devices: none -> 44.7 us  [halves_find(): lax.ppermute(value_now, shard_axis, [(dev_j, (dev_j - far_arr) % v_next)...]
    all_gather x1, waiting for transfers between devices: 45.8 us -> 23.5 us  [body(): lax.all_gather(metal_values, 'fluid', axis=0, tiled=True)]
    unnamed x49 -> x66, local copies, waits for them, and re-layouts: 30.1 us -> 38.4 us
    unnamed x13 -> x12, waiting for transfers between devices: 131 us -> 131 us
  transfers between devices with their start and end apart: 12 -> 17, of which waited for: 12 -> 17; matrix products, arithmetic and copies ran while one was open for 5% -> 5% of each run, Pallas kernels for 0% -> 0%
where the time goes in v1:
time: 1540 us; the launch traced here: 1530 us
  waiting for transfers between devices  1160 us (75%)
  local copies, waits for them, and re-layouts  216 us (14%)
  other arithmetic  59 us (4%)
  matrix products  44.9 us (3%)
  blocking collectives  24.2 us (2%)
    psum x1, waiting for transfers between devices, body(): lax.psum(jnp.stack([weight_rf, weight_vf, weight_rm, weight_vm]), 'fluid')  188 us
    pmax x1, waiting for transfers between devices, body(): col_max = lax.pmax(col_local, 'fluid')  162 us
    reduce_scatter x1, waiting for transfers between devices, body(): lax.psum_scatter(grad_rm.reshape(metal_rows, feature_cols), 'fluid', scat...  145 us
    reduce_scatter x1, waiting for transfers between devices, body(): lax.psum_scatter(num_rows, 'fluid', scatter_dimension=0, tiled=True)  145 us
    unnamed x12, waiting for transfers between devices  131 us
    reduce_scatter x1, waiting for transfers between devices, body(): lax.psum_scatter(grad_vm.reshape(metal_rows, feature_cols), 'fluid', scat...  129 us
    all_gather x1, waiting for transfers between devices, body(): lax.all_gather(metal_out, 'fluid', axis=0, tiled=True)  74.7 us
    all_gather x1, waiting for transfers between devices, body(): lax.all_gather(scaled_grad, 'fluid', axis=0, tiled=True)  72.4 us
  transfers between devices with their start and end apart: 17, of which 17 were waited for; matrix products, arithmetic and copies ran while one was open for 5% of the time, Pallas kernels for 0%

profile of v1, /device:TPU:2, one launch (start us, length us, event | category | flops | bytes accessed | tf_op | source)
XLA Modules:
  0.0 1531.7 jit_solution(14994831264107501151)
XLA Ops:
  7.2 11.8 all_gather.16
  19.8 2.9 collective-permute-start
  24.4 2.9 collective-permute-start.1
  29.5 3.1 collective-permute-start.2
  32.6 5.5 collective-permute-done.2
  38.1 4.7 collective-permute-start.3
  44.9 11.1 collective-permute-done.3
  56.8 12.9 collective-permute-done.4
  71.7 12.4 all_gather.15
  84.4 11.5 collective-permute-done.5
  103.8 3.3 reshape.334
  107.1 23.2 %while.53 = (s32[]{:T(128)}, f32[2,2,128]{2,1,0:T(2,128)S(1)}, f32[64,2,128]{2,1,0:T(2,128)S(1)}, s32[32,2]{0,1:T(2,128)S(1)}, s32[]{:T(128)}, /*index=5*/bf16[2...) while((s32[]{:T(128)}, f32[2,2,128]{2,1,0:T(2,128)S(1)}, ...), condition=%wide.region_5.6_spmd, body=%wide.region_0.5_spmd.sunk | while | flops 68692104 | bytes 3351623 | solution.py:98
  108.0 4.8 gather_fusion
  119.6 4.8 gather_fusion
  131.4 23.5 %all-gather.4.cloned.1.call-done = bf16[8192,128]{1,0:T(8,128)(2,1)} async-done(((bf16[128,128]{1,0:T(8,128)(2,1)}), bf16[8192,128]{1,0:T(8,128)(2,1)}) %all-gather.4.cloned.1.call-update) | async-done | bytes 2097168 | tf_op jit(solution)/shard_map/all_gather | solution.py:67
  155.0 8.3 reshape.335
  163.2 161.8 %all-reduce.3.cloned.1.call-done = f32[64,2,128]{2,1,0:T(2,128)} async-done(((f32[64,2,128]{2,1,0:T(2,128)}), f32[64,2,128]{2,1,0:T(2,128)}) %all-reduce.3.cloned.1.call-update) | async-done | bytes 65552 | tf_op jit(solution)/shard_map/pmax | solution.py:107
  327.5 67.4 %while.54 = (s32[]{:T(128)}, f32[2,2,128]{2,1,0:T(2,128)S(1)}, f32[2,128,2,64]{1,3,2,0:T(8,128)S(1)}, f32[64,2,128]{2,1,0:T(2,128)S(1)}, f32[64,128,2,64]{1,3,2,...) while((s32[]{:T(128)}, f32[2,2,128]{2,1,0:T(2,128)S(1)}, ...), condition=%wide.region_14.15_spmd, body=%wide.region_7.14_spmd.sunk | while | flops 209717376 | bytes 25437748 | solution.py:135
  330.5 4.8 gather_fusion.6
  335.3 5.7 gather_fusion.4
  343.7 3.6 gather_fusion.5
  347.4 3.2 fusion.127
  357.7 3.4 scatter_fusion.5
  363.9 4.8 gather_fusion.6
  368.7 5.7 gather_fusion.4
  377.2 3.6 gather_fusion.5
  380.8 3.2 fusion.127
  391.2 3.4 scatter_fusion.5
  397.7 4.6 copy.105
  402.3 5.2 copy.186
  408.4 130.0 %reduce-scatter.19.cloned.1.call-done = f32[128,2]{1,0:T(8,128)} async-done(((f32[8192,2]{1,0:T(8,128)}), f32[128,2]{1,0:T(8,128)}) %reduce-scatter.19.cloned.1.call-update) | async-done | bytes 1040
  539.3 145.3 %reduce-scatter.9.cloned.1.call-done = f32[128,128]{0,1:T(8,128)} async-done(((f32[8192,128]{0,1:T(8,128)}), f32[128,128]{0,1:T(8,128)}) %reduce-scatter.9.cloned.1.call-update) | async-done | bytes 65552 | tf_op jit(solution)/shard_map/reduce_scatter | solution.py:154
  687.1 72.4 %all-gather.6.cloned.1.call-done = bf16[8192,128]{0,1:T(8,128)(2,1)} async-done(((bf16[128,128]{0,1:T(8,128)(2,1)}), bf16[8192,128]{0,1:T(8,128)(2,1)}) %all-gather.6.cloned.1.call-update) | async-done | bytes 2097168 | tf_op jit(solution)/shard_map/all_gather | solution.py:168
  759.6 74.7 %all-gather.8.cloned.1.call-done = bf16[8192,128]{0,1:T(8,128)(2,1)} async-done(((bf16[128,128]{0,1:T(8,128)(2,1)}), bf16[8192,128]{0,1:T(8,128)(2,1)}) %all-gather.8.cloned.1.call-update) | async-done | bytes 2097168 | tf_op jit(solution)/shard_map/all_gather | solution.py:169
  834.3 2.7 multiply_bitcast_fusion
  844.4 5.2 copy.114
  854.5 131.8 %while.55 = (s32[]{:T(128)}, f32[2,128,2,64]{1,3,2,0:T(8,128)S(1)}, f32[2,128,2,64]{1,3,2,0:T(8,128)S(1)}, f32[64,128,2,64]{1,3,2,0:T(8,128)}, f32[64,128,2,64]{...) while((s32[]{:T(128)}, f32[2,128,2,64]{1,3,2,0:T(8,128)S(1)}, ...), condition=%wide.region_24.25_spmd, body=%wide.region_19.24_spmd.sunk | while | flops 482347136 | bytes 61189336 | solution.py:248
  860.9 4.8 gather_fusion.11
  867.6 4.8 gather_fusion.10
  872.4 5.7 gather_fusion.8
  880.5 3.6 gather_fusion.13
  884.1 3.6 gather_fusion.12
  890.0 3.6 gather_fusion.9
  900.4 2.9 convolution_bitcast_fusion.15
  913.6 3.4 scatter_fusion.8
  917.0 3.4 scatter_fusion.9
  926.6 4.8 gather_fusion.11
  933.3 4.8 gather_fusion.10
  938.1 5.7 gather_fusion.8
  946.2 3.6 gather_fusion.13
  949.8 3.6 gather_fusion.12
  955.7 3.6 gather_fusion.9
  966.1 2.9 convolution_bitcast_fusion.15
  979.3 3.4 scatter_fusion.8
  982.7 3.4 scatter_fusion.9
  986.3 4.6 copy.119
  990.9 5.2 copy.184
  996.2 4.6 copy.118
  1000.9 5.3 copy.185
  1008.8 129.5 %reduce-scatter.15.cloned.1.call-done = f32[128,128]{0,1:T(8,128)} async-done(((f32[8192,128]{0,1:T(8,128)}), f32[128,128]{0,1:T(8,128)}) %reduce-scatter.15.cloned.1.call-update) | async-done | bytes 65552 | tf_op jit(solution)/shard_map/reduce_scatter | solution.py:270
  1139.4 145.4 %reduce-scatter.13.cloned.1.call-done = f32[128,128]{0,1:T(8,128)} async-done(((f32[8192,128]{0,1:T(8,128)}), f32[128,128]{0,1:T(8,128)}) %reduce-scatter.13.cloned.1.call-update) | async-done | bytes 65552 | tf_op jit(solution)/shard_map/reduce_scatter | solution.py:267
  1289.7 21.0 %reduce-scatter.11.cloned.1.call-done = f32[256,128]{1,0:T(8,128)} async-done(((f32[256,512]{1,0:T(8,128)}), f32[256,128]{1,0:T(8,128)}) %reduce-scatter.11.cloned.1.call-update) | async-done | bytes 131088 | tf_op jit(solution)/shard_map/reduce_scatter | solution.py:277
  1312.2 187.8 %all-reduce.5.cloned.1.call-done = f32[4,512,128]{1,2,0:T(8,128)} async-done(((f32[4,512,128]{1,2,0:T(8,128)}), f32[4,512,128]{1,2,0:T(8,128)}) %all-reduce.5.cloned.1.call-update) | async-done | bytes 1048592 | tf_op jit(solution)/shard_map/psum | solution.py:280
  1502.6 20.8 %reduce-scatter.17.cloned.1.call-done = f32[128,128]{1,0:T(8,128)} async-done(((f32[128,512]{1,0:T(8,128)}), f32[128,128]{1,0:T(8,128)}) %reduce-scatter.17.cloned.1.call-update) | async-done | bytes 65552 | tf_op jit(solution)/shard_map/reduce_scatter | solution.py:278
  (261 shorter events, 152.5 us)
Async XLA Ops:
  7.2 11.8 copy-start
  7.2 147.8 %all-gather.4.cloned.1.call-start = ((), (), s32[]{:S(2)}) async-start(), calls=%async_computation.6 | async-start | bytes 2129920 | tf_op jit(solution)/shard_map/all_gather | solution.py:67
  19.0 51.7 %copy-start.8 = (bf16[128,512]{1,0:T(8,128)(2,1)}, bf16[128,512]{1,0:T(8,128)(2,1)S(1)}, u32[]{:S(2)}) copy-start(bf16[128,512]{1,0:T(8,128)(2,1)S(1)} %all_gather.16) | copy-start | bytes 393220
  19.8 4.5 collective-permute-start
  24.4 5.1 collective-permute-start.1
  29.4 41.3 %copy-start.17 = (bf16[512,128]{1,0:T(8,128)(2,1)S(1)}, bf16[512,128]{1,0:T(8,128)(2,1)}, u32[]{:S(2)}) copy-start(bf16[512,128]{1,0:T(8,128)(2,1)} %param.21) | copy-start | bytes 393220
  29.5 8.6 collective-permute-start.2
  38.1 33.6 %copy-start.29 = (bf16[256,128]{1,0:T(8,128)(2,1)S(1)}, bf16[256,128]{1,0:T(8,128)(2,1)}, u32[]{:S(2)}) copy-start(bf16[256,128]{1,0:T(8,128)(2,1)} %param.16) | copy-start | bytes 196612
  38.1 17.8 %collective-permute-start.3 = (bf16[1024,128]{1,0:T(8,128)(2,1)S(1)}, bf16[1024,128]{1,0:T(8,128)(2,1)S(1)}, u32[]{:S(2)}, u32[]{:S(2)}) collective-permute-start(bf16[1024,128]{1,0:T(8,128)(2,1)S(1)} %pad_maximum_fusion.1), channel_id=1, source_target_pairs={{0,224},{4,228},{8,232},{12,236},{16,240},{20,244},{24,248},{28,25... | collective-permute-start | bytes 786440 | tf_op jit(solution)/shard_map/ppermute | solution.py:19
  43.5 40.6 %copy-start.15 = (bf16[512,128]{1,0:T(8,128)(2,1)S(1)}, bf16[512,128]{1,0:T(8,128)(2,1)}, u32[]{:S(2)}) copy-start(bf16[512,128]{1,0:T(8,128)(2,1)} %param.18) | copy-start | bytes 393220
  56.8 12.9 collective-permute-start.4
  70.8 25.1 %collective-permute-start.5 = (bf16[4096,128]{1,0:T(8,128)(2,1)}, bf16[4096,128]{1,0:T(8,128)(2,1)S(1)}, u32[]{:S(2)}, u32[]{:S(2)}) collective-permute-start(bf16[4096,128]{1,0:T(8,128)(2,1)} %get-tuple-element.835), channel_id=1, source_target_pairs={{0,128},{4,132},{8,136},{12,140},{16,144},{20,148},{24,152},{28,15... | collective-permute-start | bytes 3145736 | tf_op jit(solution)/shard_map/ppermute | solution.py:19
  71.6 253.4 %all-reduce.3.cloned.1.call-start = ((), (), s32[]{:S(2)}) async-start(), calls=%async_computation.7 | async-start | bytes 131072 | tf_op jit(solution)/shard_map/pmax | solution.py:107
  84.0 47.1 %copy-start.6 = (bf16[256,512]{1,0:T(8,128)(2,1)}, bf16[256,512]{1,0:T(8,128)(2,1)S(1)}, u32[]{:S(2)}) copy-start(bf16[256,512]{1,0:T(8,128)(2,1)S(1)} %all_gather.15) | copy-start | bytes 786436
  103.8 3.3 copy-start.24
  107.1 24.0 %copy-start.13 = (bf16[512,128]{1,0:T(8,128)(2,1)S(1)}, bf16[512,128]{1,0:T(8,128)(2,1)}, u32[]{:S(2)}) copy-start(bf16[512,128]{1,0:T(8,128)(2,1)} %param.19) | copy-start | bytes 393220
  130.4 0.6 copy-start.10
  131.1 407.3 %reduce-scatter.19.cloned.1.call-start = ((), (), s32[]{:S(2)}) async-start(), calls=%async_computation.16 | async-start | bytes 4259840
  353.9 3.9 copy-start.1
  387.3 3.9 copy-start.1
  397.6 287.0 %reduce-scatter.9.cloned.1.call-start = ((), (), s32[]{:S(2)}) async-start(), calls=%async_computation.8 | async-start | bytes 4259840 | tf_op jit(solution)/shard_map/reduce_scatter | solution.py:154
  407.5 0.8 copy-start.30
  407.5 279.3 %copy-start.22 = (bf16[256,128]{1,0:T(8,128)(2,1)S(1)}, bf16[256,128]{1,0:T(8,128)(2,1)}, u32[]{:S(2)}) copy-start(bf16[256,128]{1,0:T(8,128)(2,1)} %param.22) | copy-start | bytes 196612
  407.5 352.0 %all-gather.6.cloned.1.call-start = ((), (), s32[]{:S(2)}) async-start(), calls=%async_computation.9 | async-start | bytes 2129920 | tf_op jit(solution)/shard_map/all_gather | solution.py:168
  686.1 148.1 %all-gather.8.cloned.1.call-start = ((), (), s32[]{:S(2)}) async-start(), calls=%async_computation.10 | async-start | bytes 2129920 | tf_op jit(solution)/shard_map/all_gather | solution.py:169
  686.7 451.6 %reduce-scatter.15.cloned.1.call-start = ((), (), s32[]{:S(2)}) async-start(), calls=%async_computation.13 | async-start | bytes 4259840 | tf_op jit(solution)/shard_map/reduce_scatter | solution.py:270
  687.1 149.9 %copy-start.11 = (bf16[2,128,2,64]{1,0,3,2:T(2,128)(2,1)}, bf16[2,128,2,64]{1,0,3,2:T(2,128)(2,1)S(1)}, u32[]{:S(2)}) copy-start(bf16[2,128,2,64]{1,0,3,2:T(2,128)(2,1)S(1)} %copy.104) | copy-start | bytes 196612
  856.0 0.6 copy-start.25
  856.0 0.6 copy-start.27
  896.8 1.0 copy-start.3
  896.8 1.4 copy-start.4
  896.8 1.4 copy-start.19
  896.8 1.4 copy-start.31
  903.3 1.9 copy-start.28
  911.0 2.6 copy-start.2
  911.0 2.6 copy-start.26
  913.6 3.4 copy-start.5
  921.7 0.6 copy-start.25
  921.7 0.6 copy-start.27
  962.6 1.0 copy-start.3
  962.6 1.4 copy-start.4
  962.6 1.4 copy-start.19
  962.6 1.4 copy-start.31
  969.0 1.9 copy-start.28
  976.7 2.6 copy-start.2
  976.7 2.6 copy-start.26
  979.3 3.4 copy-start.5
  996.2 288.5 %reduce-scatter.13.cloned.1.call-start = ((), (), s32[]{:S(2)}) async-start(), calls=%async_computation.12 | async-start | bytes 4259840 | tf_op jit(solution)/shard_map/reduce_scatter | solution.py:267
  1006.1 0.9 copy-start.16
  1006.1 1.2 copy-start.14
  1006.2 2.3 copy-start.7
  1006.2 304.5 %reduce-scatter.11.cloned.1.call-start = ((), (), s32[]{:S(2)}) async-start(), calls=%async_computation.11 | async-start | bytes 655360 | tf_op jit(solution)/shard_map/reduce_scatter | solution.py:277
  1006.2 132.1 %copy-start.9 = (bf16[128,512]{1,0:T(8,128)(2,1)S(1)}, bf16[128,512]{1,0:T(8,128)(2,1)}, u32[]{:S(2)}) copy-start(bf16[128,512]{1,0:T(8,128)(2,1)} %copy-done.8) | copy-start | bytes 393220
  1008.4 491.6 %all-reduce.5.cloned.1.call-start = ((), (), s32[]{:S(2)}) async-start(), calls=%async_computation.15 | async-start | bytes 2097152 | tf_op jit(solution)/shard_map/psum | solution.py:280
  1139.3 147.9 %copy-start.18 = (bf16[512,128]{1,0:T(8,128)(2,1)S(1)}, bf16[512,128]{1,0:T(8,128)(2,1)}, u32[]{:S(2)}) copy-start(bf16[512,128]{1,0:T(8,128)(2,1)} %param.21) | copy-start | bytes 393220
  1139.3 147.9 %copy-start.23 = (f32[128,128]{0,1:T(8,128)S(1)}, f32[128,128]{0,1:T(8,128)}, u32[]{:S(2)}) copy-start(f32[128,128]{0,1:T(8,128)} %reduce-scatter.15.cloned.1.call-done) | copy-start | bytes 196612
  1284.7 2.3 copy-start.21
  1285.8 2.4 copy-start.12
  1285.8 3.1 copy-start.20
  1286.9 236.4 %reduce-scatter.17.cloned.1.call-start = ((), (), s32[]{:S(2)}) async-start(), calls=%async_computation.14 | async-start | bytes 327680 | tf_op jit(solution)/shard_map/reduce_scatter | solution.py:278
Sparse Core Ops, SparseCore 0:
  71.7 83.2 all-gather.3
  159.0 165.9 all-reduce.2
  397.7 140.6 reduce-scatter.18
  542.4 142.2 reduce-scatter.8
  687.9 71.5 all-gather.5
  762.9 71.3 all-gather.7
  996.3 141.9 reduce-scatter.14
  1142.4 142.2 reduce-scatter.12
  1287.4 23.1 reduce-scatter.10
  1314.9 185.1 all-reduce.4
  1502.6 20.7 reduce-scatter.16
